TPU v7x, 256 devices: a whole 4x4x8 slice. The times are simulated.
256 devices in a mesh: grp: 16 (over x_lo, z), sp: 16 (over y, x_hi, core).
Axes of the slice: x: 4 (x_hi: 2, x_lo: 2; x = x_hi * 2 + x_lo), y: 4, z: 8, core: 2. Of those that a mesh axis runs over, the one named last changes fastest.
Arguments:
- query: bfloat16 [32768, 6144], P(('grp', 'sp')), may hold values from -160 to 160
- key: bfloat16 [32768, 512], P(('grp', 'sp')), may hold values from -160 to 160
- value: bfloat16 [32768, 512], P(('grp', 'sp')), may hold values from -6 to 6
- grad_out: bfloat16 [32768, 6144], P(('grp', 'sp')), may hold values from -64 to 64
- segment_ids: int32 [32768], P(('grp', 'sp')), may hold values from 0 to 63, never falling along the last dimension, each value on 1 to 2048 neighbouring positions
Outputs:
- grad_query: bfloat16 [32768, 6144], P(('grp', 'sp'))
- grad_key: bfloat16 [32768, 512], P(('grp', 'sp'))
- grad_value: bfloat16 [32768, 512], P(('grp', 'sp'))
Inputs may be any that keep to these rules, and one draw needn't show every extreme that they name: `segment_ids`: ids never fall along the tokens; each document (run of one id) has at most 2048 tokens, and one has exactly 2048.
All inputs are finite; a program needn't handle non-finite values.
Results may differ from a plain program's by a relative error of at most 0.012.
Values may be sent and summed in bfloat16 or wider, within the bound.
A program may use at most 128 MiB of HBM per device.

v0:
```python
import functools

import jax
import jax.numpy as jnp
from jax import lax
from jax.experimental import pallas as pl
from jax.experimental.pallas import tpu as pltpu
from jax.sharding import PartitionSpec as P

QUERY_HEADS = 48
KEY_VALUE_HEADS = 4
HEAD_SIZE = 128
TOK = 128
N_SP = 16
N_GRP = 16
ROWS = 2 * TOK
SEQ = TOK * N_SP
HALF_Q = QUERY_HEADS * HEAD_SIZE // 2
HALF_KV = KEY_VALUE_HEADS * HEAD_SIZE // 2
CORE_HEADS = QUERY_HEADS // 2
GROUP_HEADS = QUERY_HEADS // KEY_VALUE_HEADS
SCALE = HEAD_SIZE**-0.5
EXP2_SCALE = SCALE * 1.4426950408889634
NEG = -1e30
HB = 4
GROUPS = GROUP_HEADS // HB
KB = 256
ROW_KEYS = 4 * TOK
WIDE = HB * ROWS
ALL = GROUP_HEADS * ROWS
ITEMS = float(TOK * N_SP * N_GRP * (QUERY_HEADS + 2 * KEY_VALUE_HEADS) * HEAD_SIZE)

f32 = jnp.float32
bf16 = jnp.bfloat16
MESH = pl.DeviceIdType.MESH


def greet(axis, me, count):
    barrier = pltpu.get_barrier_semaphore()

    def one(d, z):
        other = lax.rem(me + d, count)
        pl.semaphore_signal(barrier, inc=1, device_id={axis: other}, device_id_type=MESH)
        return z

    lax.fori_loop(1, count, one, 0)


def span(index, size):
    return pl.ds(pl.multiple_of(index * size, size), size)


def nt(a, b):
    return lax.dot_general(a, b, (((1,), (1,)), ((), ())), preferred_element_type=f32)


def nn(a, b):
    return lax.dot_general(a, b, (((1,), (0,)), ((), ())), preferred_element_type=f32)


def columns(h, j):
    return span(h * GROUP_HEADS + j, HEAD_SIZE)


def ids_of(seg, index):
    return jnp.broadcast_to(seg[index].astype(f32), (TOK, TOK)).T


def prepare(h, row, seg, kt, kaug):
    lane = lax.broadcasted_iota(jnp.int32, (TOK, TOK), 1).astype(f32)
    for n in range(4):
        part = span(4 * row + n, TOK)
        kt[:, part] = kaug[h, part, 0:HEAD_SIZE].T
        kaug[h, part, HEAD_SIZE:] = jnp.where(ids_of(seg, 4 * row + n) == lane, 0.0, NEG).astype(bf16)


def scores(h, row, chip, diagonal, q, do, v, kaug, qoh, e_s, dp_s, top_s, stat_s):
    for t in range(GROUPS):
        wide = slice(t * WIDE, (t + 1) * WIDE)
        cols = [columns(h, t * HB + j) for j in range(HB)]
        qt = jnp.concatenate([q[:, c] for c in cols], axis=0)
        dt = jnp.concatenate([do[:, c] for c in cols], axis=0)
        qa = jnp.concatenate([qt, jnp.concatenate([qoh[...]] * HB, axis=0)], axis=1)
        top = None if diagonal else stat_s[0:1, wide]
        total = None if diagonal else stat_s[1:2, wide]
        delta = None if diagonal else stat_s[2:3, wide]
        for n in range(ROW_KEYS // KB):
            block = row * (ROW_KEYS // KB) + n
            part = span(block, KB)
            s = nt(kaug[h, part, :], qa)
            dp = nt(v[h, part, :], dt)
            if diagonal:
                place = lax.broadcasted_iota(jnp.int32, (KB, WIDE), 0) + block * KB
                token = lax.broadcasted_iota(jnp.int32, (1, ROWS), 1) + chip * ROWS
                s = jnp.where(place <= jnp.concatenate([token] * HB, axis=1), s, NEG)
            high = jnp.max(s, axis=0, keepdims=True)
            if top is not None:
                high = jnp.maximum(top, high)
                fade = jnp.exp2((top - high) * EXP2_SCALE)
            e = jnp.exp2((s - high) * EXP2_SCALE)
            e_sum = jnp.sum(e, axis=0, keepdims=True)
            d_sum = jnp.sum(e * dp, axis=0, keepdims=True)
            total = e_sum if total is None else total * fade + e_sum
            delta = d_sum if delta is None else delta * fade + d_sum
            top = high
            e_s[part, wide] = e.astype(bf16)
            dp_s[part, wide] = dp.astype(bf16)
            top_s[pl.ds(block, 1), wide] = high
        stat_s[0:1, wide] = top
        stat_s[1:2, wide] = total
        stat_s[2:3, wide] = delta


def grads(h, row, q, do, kt, e_s, dp_s, top_s, stat_s, dqt_s, dk_out, dv_out):
    qt = jnp.concatenate([q[:, columns(h, j)] for j in range(GROUP_HEADS)], axis=0)
    dt = jnp.concatenate([do[:, columns(h, j)] for j in range(GROUP_HEADS)], axis=0)
    top = stat_s[0:1, :]
    inverse = 1.0 / stat_s[1:2, :]
    delta = (stat_s[2:3, :] * inverse).astype(bf16)
    for n in range(ROW_KEYS // KB):
        block = row * (ROW_KEYS // KB) + n
        part = span(block, KB)
        weight = jnp.exp2((top_s[pl.ds(block, 1), :] - top) * EXP2_SCALE) * inverse
        p = e_s[part, :] * weight.astype(bf16)
        ds = p * (dp_s[part, :] - delta)
        dv_out[h, part, :] = nn(p, dt).astype(bf16)
        dk_out[h, part, :] = (nn(ds, qt) * SCALE).astype(bf16)
        dqt_s[...] += nn(kt[:, part], ds)


def kernel(
    q, do, k, v, seg, dq_out, k_sum, v_sum, factor,
    q2, do2, v2, seg2, dq2, e_s, dp_s, top_s, stat_s, dqt_s, kt, kaug, qoh, dk_out, dv_out,
    dq_in, dk_in, dv_in, sq_mine, sq_sp, sq_grp,
    here, near_send, near_recv, far_send, far_recv, back_send, back_recv, dq_send, dq_recv,
    sp_send, sp_recv, grp_send, grp_recv,
):
    me = lax.axis_index("sp")
    group = lax.axis_index("grp")
    core = lax.rem(me, 2)
    chip = me // 2
    row = me // 4
    peer = me + 1 - 2 * core

    def remote(src, dst, send, recv, target):
        return pltpu.make_async_remote_copy(
            src_ref=src, dst_ref=dst, send_sem=send, recv_sem=recv, device_id={"sp": target}, device_id_type=MESH
        )

    def near(h):
        lanes = span((1 - core) * 2 + h, HALF_Q // 2)
        to = span(h, HALF_Q // 2)
        return [
            remote(a.at[:, lanes], b.at[span(core, TOK), to], near_send.at[n, h], near_recv.at[n, h], peer)
            for n, (a, b) in enumerate(((q, q2), (do, do2)))
        ]

    def far(h, src, target):
        lanes = span(lax.rem(target, 2) * 2 + h, HEAD_SIZE)
        part = span(src, TOK)
        return [
            remote(a.at[:, lanes], b, far_send.at[n, h, target], far_recv.at[n, h, src], target)
            for n, (a, b) in enumerate(((k, kaug.at[h, part, 0:HEAD_SIZE]), (v, v2.at[h, part, :])))
        ]

    def ids(src, target):
        return remote(seg, seg2.at[src], far_send.at[2, 0, target], far_recv.at[2, 0, src], target)

    def back(h, src, target):
        part = span(target, TOK)
        return [
            remote(a.at[h, part, :], b.at[src, h], back_send.at[n, h, target], back_recv.at[n, h, src], target)
            for n, (a, b) in enumerate(((dk_out, dk_in), (dv_out, dv_in)))
        ]

    def back_near(h):
        lanes = span(h, HALF_Q // 2)
        return remote(dq2.at[span(1 - core, TOK), lanes], dq_in.at[:, lanes], dq_send.at[h], dq_recv.at[h], peer)

    greet("sp", me, N_SP)
    greet("grp", group, N_GRP)
    def local(h):
        half = span(core * 2 + h, HALF_Q // 2)
        to = span(h, HALF_Q // 2)
        lanes = span(core * 2 + h, HEAD_SIZE)
        return [
            pltpu.make_async_copy(q.at[:, half], q2.at[span(core, TOK), to], here.at[0, h]),
            pltpu.make_async_copy(do.at[:, half], do2.at[span(core, TOK), to], here.at[1, h]),
            pltpu.make_async_copy(k.at[:, lanes], kaug.at[h, span(me, TOK), 0:HEAD_SIZE], here.at[2, h]),
            pltpu.make_async_copy(v.at[:, lanes], v2.at[h, span(me, TOK), :], here.at[3, h]),
        ]

    own_ids = pltpu.make_async_copy(seg, seg2.at[me], here.at[4, 0])
    own_ids.start()
    pl.semaphore_wait(pltpu.get_barrier_semaphore(), N_SP + N_GRP - 2)

    def send_all(h, z):
        for copy in near(h):
            copy.start()
        for copy in local(h):
            copy.start()

        def send(d, z):
            target = lax.rem(me + d, N_SP)

            @pl.when(target // 4 >= row)
            def _():
                for copy in far(h, me, target):
                    copy.start()

                @pl.when(h == 0)
                def _():
                    ids(me, target).start()

            return z

        return lax.fori_loop(1, N_SP, send, z)

    lax.fori_loop(0, 2, send_all, 0)
    own_ids.wait()
    lane = lax.broadcasted_iota(jnp.int32, (TOK, TOK), 1).astype(f32)

    def head(h, z):
        for copy in local(h):
            copy.wait()
        for copy in near(h):
            copy.wait_recv()

        def arrive(at):
            def one(n, z):
                other = 4 * at + n

                @pl.when(other != me)
                def _():
                    for copy in far(h, other, me):
                        copy.wait_recv()

                    @pl.when(h == 0)
                    def _():
                        ids(other, me).wait_recv()

                return z

            lax.fori_loop(0, 4, one, 0)
            prepare(h, at, seg2, kt, kaug)

        arrive(row)

        @pl.when(h == 0)
        def _():
            for c in range(2):
                hot = jnp.where(ids_of(seg2, 2 * chip + c) == lane, 1.0, 0.0)
                qoh[c * TOK : (c + 1) * TOK, :] = hot.astype(bf16)

        common = (q2, do2, v2, kaug, qoh, e_s, dp_s, top_s, stat_s)
        scores(h, row, chip, True, *common)

        def earlier(d, z):
            arrive(row - d)
            scores(h, row - d, chip, False, *common)
            return z

        lax.fori_loop(1, row + 1, earlier, 0)
        dqt_s[...] = jnp.zeros_like(dqt_s)

        def backward(at, z):
            grads(h, at, q2, do2, kt, e_s, dp_s, top_s, stat_s, dqt_s, dk_out, dv_out)

            def give(n, z):
                target = 4 * at + n

                @pl.when((target // 2 <= chip) & (target != me))
                def _():
                    for copy in back(h, me, target):
                        copy.start()

                return z

            return lax.fori_loop(0, 4, give, z)

        lax.fori_loop(0, row + 1, backward, 0)
        for j in range(GROUP_HEADS):
            out = dqt_s[:, j * ROWS : (j + 1) * ROWS] * SCALE
            dq2[:, columns(h, j)] = out.T.astype(bf16)
        back_near(h).start()
        return z

    lax.fori_loop(0, 2, head, 0)

    def square(x):
        x = x.astype(f32)
        return jnp.sum(x * x)

    def settle(d, z):
        other = lax.rem(me + d, N_SP)

        @pl.when(other // 4 >= row)
        def _():
            for h in range(2):
                for copy in far(h, me, other):
                    copy.wait_send()
            ids(me, other).wait_send()

        return z

    lax.fori_loop(1, N_SP, settle, 0)
    for h in range(2):
        for copy in near(h):
            copy.wait_send()
    own = dq2.at[span(core, TOK), :]
    out = [
        pltpu.make_async_copy(own, dq_out.at[:, span(core, HALF_Q)], here.at[0, 0]),
        pltpu.make_async_copy(dq_in, dq_out.at[:, span(1 - core, HALF_Q)], here.at[1, 0]),
    ]
    out[0].start()
    squares = square(own[...])

    def halves(g, z):
        back_near(g).wait()
        return z

    lax.fori_loop(0, 2, halves, 0)
    out[1].start()
    squares += square(dq_in[...])
    for c in range(2):
        for h in range(2):
            lanes = slice((2 * c + h) * HEAD_SIZE, (2 * c + h + 1) * HEAD_SIZE)
            k_sum[:, lanes] = jnp.zeros((TOK, HEAD_SIZE), f32)
            v_sum[:, lanes] = jnp.zeros((TOK, HEAD_SIZE), f32)

            @pl.when(core == c)
            def _():
                k_sum[:, lanes] = dk_out[h, span(me, TOK), :].astype(f32)
                v_sum[:, lanes] = dv_out[h, span(me, TOK), :].astype(f32)

    for h in range(2):

        def add(j, z):
            for c in range(2):
                other = 2 * j + c

                @pl.when(other != me)
                def _():
                    for copy in back(h, other, me):
                        copy.wait_recv()
                    lanes = slice((2 * c + h) * HEAD_SIZE, (2 * c + h + 1) * HEAD_SIZE)
                    k_sum[:, lanes] += dk_in[other, h].astype(f32)
                    v_sum[:, lanes] += dv_in[other, h].astype(f32)

            return z

        lax.fori_loop(chip, N_SP // 2, add, 0)
    squares += square(k_sum[...]) + square(v_sum[...])
    for axis, index, count, slots, sends, recvs in (
        ("sp", me, N_SP, sq_sp, sp_send, sp_recv),
        ("grp", group, N_GRP, sq_grp, grp_send, grp_recv),
    ):
        stage = 0 if axis == "sp" else 1
        sq_mine[stage] = jnp.full((8, 128), squares, f32)

        def message(src, target):
            return pltpu.make_async_remote_copy(
                src_ref=sq_mine.at[stage],
                dst_ref=slots.at[src],
                send_sem=sends.at[target],
                recv_sem=recvs.at[src],
                device_id={axis: target},
                device_id_type=MESH,
            )

        def start(d, z):
            message(index, lax.rem(index + d, count)).start()
            return z

        def wait(d, z):
            other = lax.rem(index + d, count)
            message(index, other).wait_send()
            message(other, index).wait_recv()
            return z

        lax.fori_loop(1, count, start, 0)
        slots[index] = sq_mine[stage]
        lax.fori_loop(1, count, wait, 0)
        tile = jnp.sum(slots[...], axis=0)
        squares = jnp.max(tile)

    def given(d, z):
        target = lax.rem(me + d, N_SP)

        @pl.when(target // 2 <= chip)
        def _():
            for h in range(2):
                for copy in back(h, me, target):
                    copy.wait_send()

        return z

    lax.fori_loop(1, N_SP, given, 0)
    factor[...] = 1.0 / jnp.sqrt(jnp.full((8, 128), squares, f32) / ITEMS + 1e-6)
    for copy in out:
        copy.wait()


def scale_kernel(dq, dk, dv, factor, gq, gk, gv):
    by = factor[0:1, 0:1]
    gq[...] = (dq[...].astype(f32) * by).astype(bf16)

    @pl.when(pl.program_id(0) == 0)
    def _():
        gk[...] = (dk[...] * by).astype(bf16)
        gv[...] = (dv[...] * by).astype(bf16)


def scale(dq, dk, dv, factor):
    steps = 4
    part = pl.BlockSpec((TOK // steps, dq.shape[1]), lambda i: (i, 0))
    whole = pl.BlockSpec(dk.shape, lambda i: (0, 0))
    return pl.pallas_call(
        scale_kernel,
        grid=(steps,),
        out_shape=tuple(jax.ShapeDtypeStruct(x.shape, bf16) for x in (dq, dk, dv)),
        in_specs=[part, whole, whole, pl.BlockSpec((8, 128), lambda i: (0, 0))],
        out_specs=[part, whole, whole],
        name="scale",
    )(dq, dk, dv, factor)


def on_device(query, key, value, grad_out, segment_ids):
    vmem = pltpu.VMEM
    sems = pltpu.SemaphoreType.DMA
    width = KEY_VALUE_HEADS * HEAD_SIZE
    dq, dk, dv, factor = pl.pallas_call(
        kernel,
        out_shape=(
            jax.ShapeDtypeStruct((TOK, QUERY_HEADS * HEAD_SIZE), bf16),
            jax.ShapeDtypeStruct((TOK, width), f32),
            jax.ShapeDtypeStruct((TOK, width), f32),
            jax.ShapeDtypeStruct((8, 128), f32),
        ),
        in_specs=[pl.BlockSpec(memory_space=pl.ANY)] * 5,
        out_specs=[pl.BlockSpec(memory_space=pl.ANY)] + [pl.BlockSpec(memory_space=vmem)] * 3,
        scratch_shapes=[
            vmem((ROWS, HALF_Q), bf16),
            vmem((ROWS, HALF_Q), bf16),
            vmem((2, SEQ, HEAD_SIZE), bf16),
            vmem((N_SP, 1, TOK), jnp.int32),
            vmem((ROWS, HALF_Q), bf16),
            vmem((SEQ, ALL), bf16),
            vmem((SEQ, ALL), bf16),
            vmem((8, ALL), f32),
            vmem((8, ALL), f32),
            vmem((HEAD_SIZE, ALL), f32),
            vmem((HEAD_SIZE, SEQ), bf16),
            vmem((2, SEQ, 2 * HEAD_SIZE), bf16),
            vmem((ROWS, HEAD_SIZE), bf16),
            vmem((2, SEQ, HEAD_SIZE), bf16),
            vmem((2, SEQ, HEAD_SIZE), bf16),
            vmem((TOK, HALF_Q), bf16),
            vmem((N_SP, 2, TOK, HEAD_SIZE), bf16),
            vmem((N_SP, 2, TOK, HEAD_SIZE), bf16),
            vmem((2, 8, 128), f32),
            vmem((N_SP, 8, 128), f32),
            vmem((N_GRP, 8, 128), f32),
            sems((5, 2)),
            sems((2, 2)),
            sems((2, 2)),
            sems((3, 2, N_SP)),
            sems((3, 2, N_SP)),
            sems((2, 2, N_SP)),
            sems((2, 2, N_SP)),
            sems((2,)),
            sems((2,)),
            sems((N_SP,)),
            sems((N_SP,)),
            sems((N_GRP,)),
            sems((N_GRP,)),
        ],
        compiler_params=pltpu.CompilerParams(
            collective_id=0, has_side_effects=True, vmem_limit_bytes=58 << 20
        ),
        name="attention_grads",
    )(query, grad_out, key, value, segment_ids.reshape(1, TOK))
    return scale(dq, dk, dv, factor)


def solution(mesh):
    whole = P(("grp", "sp"), None)
    return jax.shard_map(
        on_device,
        mesh=mesh,
        in_specs=(whole, whole, whole, whole, P(("grp", "sp"))),
        out_specs=(whole, whole, whole),
        check_vma=False,
    )
```

profile of v0, /device:TPU:1, one launch (start us, length us, event | category | flops | bytes accessed | tf_op | source)
XLA Modules:
  0.0 91.5 jit_solution(11358614630260122509)
XLA Ops:
  0.6 86.8 %attention_grads.1 = (bf16[128,6144]{1,0:T(8,128)(2,1)}, f32[128,512]{1,0:T(8,128)}, f32[128,512]{1,0:T(8,128)}, f32[8,128]{1,0:T(8,128)}) custom-call(bf16[128,6144]{1,0:T(8,128)(2,1)} %q.1, bf16[128,6144]{1,0:T(8,128)(2,1)} %do.1, bf16[128,512]{1,0:T(8,128)(2,1)} %k.1, bf16[128,512]{1,0:T(8,128)(2,1)} %v.1, s32[1,128]{1,0:T(1,128)} %bitcast.1), custom_call_target="tpu_custom_call" | custom-call | tf_op jit(solution)/shard_map/attention_grads/pallas_call | solution.py:432
  87.4 4.1 %scale.1 = (bf16[128,6144]{1,0:T(8,128)(2,1)}, bf16[128,512]{1,0:T(8,128)(2,1)}, bf16[128,512]{1,0:T(8,128)(2,1)}) custom-call(bf16[128,6144]{1,0:T(8,128)(2,1)} %get-tuple-element.7.dq, f32[128,512]{1,0:T(8,128)} %get-tuple-element.8.dk, f32[128,512]{1,0:T(8,128)} %get-tuple-element.9.dv, f32[8,128]{1,0:T(8,128)} %get-tuple-element.10.factor), custom_call_target="tpu_custom_call" | custom-call | tf_op jit(solution)/shard_map/scale/pallas_call | solution.py:418
where the time goes:
time: 91.6 us; the launch traced here: 91.5 us
  Pallas kernels  90.8 us (99%)
    pallas_call x1, Pallas kernels, on_device(): pl.pallas_call(kernel, out_shape=(jax.ShapeDtypeStruct((TOK, QUERY_HEADS...  86.8 us
    pallas_call x1, Pallas kernels, scale(): pl.pallas_call(scale_kernel, grid=(steps,), out_shape=tuple((jax.ShapeDty...  4.06 us

commit v1 on v0

--- a/solution.py
+++ b/solution.py
@@ -24,8 +24,8 @@
 NEG = -1e30
 HB = 4
 GROUPS = GROUP_HEADS // HB
-KB = 256
 ROW_KEYS = 4 * TOK
+STEPS = 8
 WIDE = HB * ROWS
 ALL = GROUP_HEADS * ROWS
 ITEMS = float(TOK * N_SP * N_GRP * (QUERY_HEADS + 2 * KEY_VALUE_HEADS) * HEAD_SIZE)
@@ -67,46 +67,49 @@
 
 
 def prepare(h, row, seg, kt, kaug):
-    lane = lax.broadcasted_iota(jnp.int32, (TOK, TOK), 1).astype(f32)
     for n in range(4):
         part = span(4 * row + n, TOK)
         kt[:, part] = kaug[h, part, 0:HEAD_SIZE].T
-        kaug[h, part, HEAD_SIZE:] = jnp.where(ids_of(seg, 4 * row + n) == lane, 0.0, NEG).astype(bf16)
-
-
-def scores(h, row, chip, diagonal, q, do, v, kaug, qoh, e_s, dp_s, top_s, stat_s):
+
+    @pl.when(h == 0)
+    def _():
+        lane = lax.broadcasted_iota(jnp.int32, (TOK, TOK), 1).astype(f32)
+        for n in range(4):
+            mask = jnp.where(ids_of(seg, 4 * row + n) == lane, 0.0, NEG).astype(bf16)
+            for both in range(2):
+                kaug[both, span(4 * row + n, TOK), HEAD_SIZE:] = mask
+
+
+def scores(h, row, chip, diagonal, q, do, v, kaug, qoh, s_s, e_s, dp_s, top_s, stat_s):
+    part = span(row, ROW_KEYS)
+    tops = []
     for t in range(GROUPS):
         wide = slice(t * WIDE, (t + 1) * WIDE)
-        cols = [columns(h, t * HB + j) for j in range(HB)]
-        qt = jnp.concatenate([q[:, c] for c in cols], axis=0)
-        dt = jnp.concatenate([do[:, c] for c in cols], axis=0)
+        qt = jnp.concatenate([q[:, columns(h, t * HB + j)] for j in range(HB)], axis=0)
         qa = jnp.concatenate([qt, jnp.concatenate([qoh[...]] * HB, axis=0)], axis=1)
-        top = None if diagonal else stat_s[0:1, wide]
-        total = None if diagonal else stat_s[1:2, wide]
-        delta = None if diagonal else stat_s[2:3, wide]
-        for n in range(ROW_KEYS // KB):
-            block = row * (ROW_KEYS // KB) + n
-            part = span(block, KB)
-            s = nt(kaug[h, part, :], qa)
-            dp = nt(v[h, part, :], dt)
-            if diagonal:
-                place = lax.broadcasted_iota(jnp.int32, (KB, WIDE), 0) + block * KB
-                token = lax.broadcasted_iota(jnp.int32, (1, ROWS), 1) + chip * ROWS
-                s = jnp.where(place <= jnp.concatenate([token] * HB, axis=1), s, NEG)
-            high = jnp.max(s, axis=0, keepdims=True)
-            if top is not None:
-                high = jnp.maximum(top, high)
-                fade = jnp.exp2((top - high) * EXP2_SCALE)
-            e = jnp.exp2((s - high) * EXP2_SCALE)
-            e_sum = jnp.sum(e, axis=0, keepdims=True)
-            d_sum = jnp.sum(e * dp, axis=0, keepdims=True)
-            total = e_sum if total is None else total * fade + e_sum
-            delta = d_sum if delta is None else delta * fade + d_sum
-            top = high
-            e_s[part, wide] = e.astype(bf16)
-            dp_s[part, wide] = dp.astype(bf16)
-            top_s[pl.ds(block, 1), wide] = high
-        stat_s[0:1, wide] = top
+        s = nt(kaug[h, part, :], qa)
+        if diagonal:
+            place = lax.broadcasted_iota(jnp.int32, (ROW_KEYS, WIDE), 0) + row * ROW_KEYS
+            token = lax.broadcasted_iota(jnp.int32, (1, ROWS), 1) + chip * ROWS
+            s = jnp.where(place <= jnp.concatenate([token] * HB, axis=1), s, NEG)
+        s_s[:, wide] = s
+        high = jnp.max(s, axis=0, keepdims=True)
+        tops.append(high if diagonal else jnp.maximum(stat_s[0:1, wide], high))
+    for t, high in enumerate(tops):
+        wide = slice(t * WIDE, (t + 1) * WIDE)
+        dt = jnp.concatenate([do[:, columns(h, t * HB + j)] for j in range(HB)], axis=0)
+        dp = nt(v[h, part, :], dt)
+        e = jnp.exp2((s_s[:, wide] - high) * EXP2_SCALE)
+        total = jnp.sum(e, axis=0, keepdims=True)
+        delta = jnp.sum(e * dp, axis=0, keepdims=True)
+        if not diagonal:
+            fade = jnp.exp2((stat_s[0:1, wide] - high) * EXP2_SCALE)
+            total += stat_s[1:2, wide] * fade
+            delta += stat_s[2:3, wide] * fade
+        e_s[part, wide] = e.astype(bf16)
+        dp_s[part, wide] = dp.astype(bf16)
+        top_s[pl.ds(row, 1), wide] = high
+        stat_s[0:1, wide] = high
         stat_s[1:2, wide] = total
         stat_s[2:3, wide] = delta
 
@@ -114,23 +117,20 @@
 def grads(h, row, q, do, kt, e_s, dp_s, top_s, stat_s, dqt_s, dk_out, dv_out):
     qt = jnp.concatenate([q[:, columns(h, j)] for j in range(GROUP_HEADS)], axis=0)
     dt = jnp.concatenate([do[:, columns(h, j)] for j in range(GROUP_HEADS)], axis=0)
-    top = stat_s[0:1, :]
     inverse = 1.0 / stat_s[1:2, :]
     delta = (stat_s[2:3, :] * inverse).astype(bf16)
-    for n in range(ROW_KEYS // KB):
-        block = row * (ROW_KEYS // KB) + n
-        part = span(block, KB)
-        weight = jnp.exp2((top_s[pl.ds(block, 1), :] - top) * EXP2_SCALE) * inverse
-        p = e_s[part, :] * weight.astype(bf16)
-        ds = p * (dp_s[part, :] - delta)
-        dv_out[h, part, :] = nn(p, dt).astype(bf16)
-        dk_out[h, part, :] = (nn(ds, qt) * SCALE).astype(bf16)
-        dqt_s[...] += nn(kt[:, part], ds)
+    part = span(row, ROW_KEYS)
+    weight = jnp.exp2((top_s[pl.ds(row, 1), :] - stat_s[0:1, :]) * EXP2_SCALE) * inverse
+    p = e_s[part, :] * weight.astype(bf16)
+    ds = p * (dp_s[part, :] - delta)
+    dv_out[h, part, :] = nn(p, dt).astype(bf16)
+    dk_out[h, part, :] = (nn(ds, qt) * SCALE).astype(bf16)
+    dqt_s[...] += nn(kt[:, part], ds)
 
 
 def kernel(
     q, do, k, v, seg, dq_out, k_sum, v_sum, factor,
-    q2, do2, v2, seg2, dq2, e_s, dp_s, top_s, stat_s, dqt_s, kt, kaug, qoh, dk_out, dv_out,
+    q2, do2, v2, seg2, dq2, s_s, e_s, dp_s, top_s, stat_s, dqt_s, kt, kaug, qoh, dk_out, dv_out,
     dq_in, dk_in, dv_in, sq_mine, sq_sp, sq_grp,
     here, near_send, near_recv, far_send, far_recv, back_send, back_recv, dq_send, dq_recv,
     sp_send, sp_recv, grp_send, grp_recv,
@@ -252,7 +252,7 @@
                 hot = jnp.where(ids_of(seg2, 2 * chip + c) == lane, 1.0, 0.0)
                 qoh[c * TOK : (c + 1) * TOK, :] = hot.astype(bf16)
 
-        common = (q2, do2, v2, kaug, qoh, e_s, dp_s, top_s, stat_s)
+        common = (q2, do2, v2, kaug, qoh, s_s, e_s, dp_s, top_s, stat_s)
         scores(h, row, chip, True, *common)
 
         def earlier(d, z):
@@ -281,7 +281,7 @@
         lax.fori_loop(0, row + 1, backward, 0)
         for j in range(GROUP_HEADS):
             out = dqt_s[:, j * ROWS : (j + 1) * ROWS] * SCALE
-            dq2[:, columns(h, j)] = out.T.astype(bf16)
+            dq2[:, columns(h, j)] = out.astype(bf16).T
         back_near(h).start()
         return z
 
@@ -291,22 +291,6 @@
         x = x.astype(f32)
         return jnp.sum(x * x)
 
-    def settle(d, z):
-        other = lax.rem(me + d, N_SP)
-
-        @pl.when(other // 4 >= row)
-        def _():
-            for h in range(2):
-                for copy in far(h, me, other):
-                    copy.wait_send()
-            ids(me, other).wait_send()
-
-        return z
-
-    lax.fori_loop(1, N_SP, settle, 0)
-    for h in range(2):
-        for copy in near(h):
-            copy.wait_send()
     own = dq2.at[span(core, TOK), :]
     out = [
         pltpu.make_async_copy(own, dq_out.at[:, span(core, HALF_Q)], here.at[0, 0]),
@@ -351,12 +335,35 @@
 
         lax.fori_loop(chip, N_SP // 2, add, 0)
     squares += square(k_sum[...]) + square(v_sum[...])
-    for axis, index, count, slots, sends, recvs in (
-        ("sp", me, N_SP, sq_sp, sp_send, sp_recv),
-        ("grp", group, N_GRP, sq_grp, grp_send, grp_recv),
-    ):
-        stage = 0 if axis == "sp" else 1
-        sq_mine[stage] = jnp.full((8, 128), squares, f32)
+
+    def settle():
+        def one(d, z):
+            other = lax.rem(me + d, N_SP)
+
+            @pl.when(other // 4 >= row)
+            def _():
+                for h in range(2):
+                    for copy in far(h, me, other):
+                        copy.wait_send()
+                ids(me, other).wait_send()
+
+            @pl.when(other // 2 <= chip)
+            def _():
+                for h in range(2):
+                    for copy in back(h, me, other):
+                        copy.wait_send()
+
+            return z
+
+        lax.fori_loop(1, N_SP, one, 0)
+        for h in range(2):
+            for copy in near(h):
+                copy.wait_send()
+        for copy in out:
+            copy.wait()
+
+    def share(stage, axis, index, count, slots, sends, recvs, amount, beside):
+        sq_mine[stage] = jnp.full((8, 128), amount, f32)
 
         def message(src, target):
             return pltpu.make_async_remote_copy(
@@ -368,59 +375,65 @@
                 device_id_type=MESH,
             )
 
-        def start(d, z):
+        for d in range(1, count):
             message(index, lax.rem(index + d, count)).start()
-            return z
-
-        def wait(d, z):
-            other = lax.rem(index + d, count)
-            message(index, other).wait_send()
-            message(other, index).wait_recv()
-            return z
-
-        lax.fori_loop(1, count, start, 0)
         slots[index] = sq_mine[stage]
-        lax.fori_loop(1, count, wait, 0)
-        tile = jnp.sum(slots[...], axis=0)
-        squares = jnp.max(tile)
-
-    def given(d, z):
-        target = lax.rem(me + d, N_SP)
-
-        @pl.when(target // 2 <= chip)
-        def _():
-            for h in range(2):
-                for copy in back(h, me, target):
-                    copy.wait_send()
-
-        return z
-
-    lax.fori_loop(1, N_SP, given, 0)
+        beside()
+        for d in range(1, count):
+            message(lax.rem(index + d, count), index).wait_recv()
+
+        def sent():
+            for d in range(1, count):
+                message(index, lax.rem(index + d, count)).wait_send()
+
+        return jnp.max(jnp.sum(slots[...], axis=0)), sent
+
+    squares, sent_sp = share(0, "sp", me, N_SP, sq_sp, sp_send, sp_recv, squares, settle)
+    squares, sent_grp = share(1, "grp", group, N_GRP, sq_grp, grp_send, grp_recv, squares, sent_sp)
+    sent_grp()
     factor[...] = 1.0 / jnp.sqrt(jnp.full((8, 128), squares, f32) / ITEMS + 1e-6)
-    for copy in out:
+
+
+def scale_kernel(dq, dk, dv, factor, gq, gk, gv, x, xk, xv, by, y, yk, yv, come, go):
+    rows = TOK // STEPS
+    parts = [slice(i * rows, (i + 1) * rows) for i in range(STEPS)]
+    moves = [(dk, xk, yk, gk), (dv, xv, yv, gv)]
+    moves += [(dq.at[p, :], x.at[p, :], y.at[p, :], gq.at[p, :]) for p in parts]
+    head = pltpu.make_async_copy(factor, by, come.at[STEPS + 2])
+    head.start()
+    enter = [pltpu.make_async_copy(m[0], m[1], come.at[i]) for i, m in enumerate(moves)]
+    leave = [pltpu.make_async_copy(m[2], m[3], go.at[i]) for i, m in enumerate(moves)]
+    for copy in enter:
+        copy.start()
+    head.wait()
+    value = by[0:1, 0:1]
+    for i, m in enumerate(moves):
+        enter[i].wait()
+        m[2][...] = (m[1][...].astype(f32) * value).astype(bf16)
+        leave[i].start()
+    for copy in leave:
         copy.wait()
 
 
-def scale_kernel(dq, dk, dv, factor, gq, gk, gv):
-    by = factor[0:1, 0:1]
-    gq[...] = (dq[...].astype(f32) * by).astype(bf16)
-
-    @pl.when(pl.program_id(0) == 0)
-    def _():
-        gk[...] = (dk[...] * by).astype(bf16)
-        gv[...] = (dv[...] * by).astype(bf16)
-
-
 def scale(dq, dk, dv, factor):
-    steps = 4
-    part = pl.BlockSpec((TOK // steps, dq.shape[1]), lambda i: (i, 0))
-    whole = pl.BlockSpec(dk.shape, lambda i: (0, 0))
+    far = pl.BlockSpec(memory_space=pl.ANY)
+    vmem = pltpu.VMEM
     return pl.pallas_call(
         scale_kernel,
-        grid=(steps,),
         out_shape=tuple(jax.ShapeDtypeStruct(x.shape, bf16) for x in (dq, dk, dv)),
-        in_specs=[part, whole, whole, pl.BlockSpec((8, 128), lambda i: (0, 0))],
-        out_specs=[part, whole, whole],
+        in_specs=[far] * 4,
+        out_specs=[far] * 3,
+        scratch_shapes=[
+            vmem(dq.shape, bf16),
+            vmem(dk.shape, f32),
+            vmem(dv.shape, f32),
+            vmem(factor.shape, f32),
+            vmem(dq.shape, bf16),
+            vmem(dk.shape, bf16),
+            vmem(dv.shape, bf16),
+            pltpu.SemaphoreType.DMA((STEPS + 3,)),
+            pltpu.SemaphoreType.DMA((STEPS + 2,)),
+        ],
         name="scale",
     )(dq, dk, dv, factor)
 
@@ -445,6 +458,7 @@
             vmem((2, SEQ, HEAD_SIZE), bf16),
             vmem((N_SP, 1, TOK), jnp.int32),
             vmem((ROWS, HALF_Q), bf16),
+            vmem((ROW_KEYS, ALL), f32),
             vmem((SEQ, ALL), bf16),
             vmem((SEQ, ALL), bf16),
             vmem((8, ALL), f32),

time: 91.6 us -> 86.4 us (0.943)
  Pallas kernels: 90.8 us -> 85.6 us
    pallas_call x1, Pallas kernels: 86.8 us -> 83.2 us  [on_device(): pl.pallas_call(kernel, out_shape=(jax.ShapeDtypeStruct((TOK, QUERY_HEADS...]
    pallas_call x1, Pallas kernels: 4.06 us -> 2.44 us  [scale(): pl.pallas_call(scale_kernel, out_shape=tuple((jax.ShapeDtypeStruct(x.shap...]
where the time goes in v1:
time: 86.4 us; the launch traced here: 86.3 us
  Pallas kernels  85.6 us (99%)
    pallas_call x1, Pallas kernels, on_device(): pl.pallas_call(kernel, out_shape=(jax.ShapeDtypeStruct((TOK, QUERY_HEADS...  83.2 us
    pallas_call x1, Pallas kernels, scale(): pl.pallas_call(scale_kernel, out_shape=tuple((jax.ShapeDtypeStruct(x.shap...  2.44 us

profile of v1, /device:TPU:1, one launch (start us, length us, event | category | flops | bytes accessed | tf_op | source)
XLA Modules:
  0.0 86.3 jit_solution(14440468552088821677)
XLA Ops:
  0.6 83.2 %attention_grads.1 = (bf16[128,6144]{1,0:T(8,128)(2,1)}, f32[128,512]{1,0:T(8,128)}, f32[128,512]{1,0:T(8,128)}, f32[8,128]{1,0:T(8,128)}) custom-call(bf16[128,6144]{1,0:T(8,128)(2,1)} %q.1, bf16[128,6144]{1,0:T(8,128)(2,1)} %do.1, bf16[128,512]{1,0:T(8,128)(2,1)} %k.1, bf16[128,512]{1,0:T(8,128)(2,1)} %v.1, s32[1,128]{1,0:T(1,128)} %bitcast.1), custom_call_target="tpu_custom_call" | custom-call | tf_op jit(solution)/shard_map/attention_grads/pallas_call | solution.py:445
  83.9 2.4 %scale.1 = (bf16[128,6144]{1,0:T(8,128)(2,1)}, bf16[128,512]{1,0:T(8,128)(2,1)}, bf16[128,512]{1,0:T(8,128)(2,1)}) custom-call(bf16[128,6144]{1,0:T(8,128)(2,1)} %get-tuple-element.7.dq, f32[128,512]{1,0:T(8,128)} %get-tuple-element.8.dk, f32[128,512]{1,0:T(8,128)} %get-tuple-element.9.dv, f32[8,128]{1,0:T(8,128)} %get-tuple-element.10.factor), custom_call_target="tpu_custom_call" | custom-call | tf_op jit(solution)/shard_map/scale/pallas_call | solution.py:421

commit v2 on v1

--- a/solution.py
+++ b/solution.py
@@ -263,7 +263,8 @@
         lax.fori_loop(1, row + 1, earlier, 0)
         dqt_s[...] = jnp.zeros_like(dqt_s)
 
-        def backward(at, z):
+        def backward(step, z):
+            at = lax.rem(step + 1, row + 1)
             grads(h, at, q2, do2, kt, e_s, dp_s, top_s, stat_s, dqt_s, dk_out, dv_out)
 
             def give(n, z):

time: 86.4 us -> 85.3 us (0.987)
  Pallas kernels: 85.6 us -> 84.6 us
    pallas_call x1, Pallas kernels: 83.2 us -> 82.1 us  [on_device(): pl.pallas_call(kernel, out_shape=(jax.ShapeDtypeStruct((TOK, QUERY_HEADS...]
where the time goes in v2:
time: 85.3 us; the launch traced here: 85.2 us
  Pallas kernels  84.6 us (99%)
    pallas_call x1, Pallas kernels, on_device(): pl.pallas_call(kernel, out_shape=(jax.ShapeDtypeStruct((TOK, QUERY_HEADS...  82.1 us
    pallas_call x1, Pallas kernels, scale(): pl.pallas_call(scale_kernel, out_shape=tuple((jax.ShapeDtypeStruct(x.shap...  2.44 us

profile of v2, /device:TPU:1, one launch (start us, length us, event | category | flops | bytes accessed | tf_op | source)
XLA Modules:
  0.0 85.2 jit_solution(5940909495308454491)
XLA Ops:
  0.6 82.1 %attention_grads.1 = (bf16[128,6144]{1,0:T(8,128)(2,1)}, f32[128,512]{1,0:T(8,128)}, f32[128,512]{1,0:T(8,128)}, f32[8,128]{1,0:T(8,128)}) custom-call(bf16[128,6144]{1,0:T(8,128)(2,1)} %q.1, bf16[128,6144]{1,0:T(8,128)(2,1)} %do.1, bf16[128,512]{1,0:T(8,128)(2,1)} %k.1, bf16[128,512]{1,0:T(8,128)(2,1)} %v.1, s32[1,128]{1,0:T(1,128)} %bitcast.1), custom_call_target="tpu_custom_call" | custom-call | tf_op jit(solution)/shard_map/attention_grads/pallas_call | solution.py:446
  82.8 2.4 %scale.1 = (bf16[128,6144]{1,0:T(8,128)(2,1)}, bf16[128,512]{1,0:T(8,128)(2,1)}, bf16[128,512]{1,0:T(8,128)(2,1)}) custom-call(bf16[128,6144]{1,0:T(8,128)(2,1)} %get-tuple-element.7.dq, f32[128,512]{1,0:T(8,128)} %get-tuple-element.8.dk, f32[128,512]{1,0:T(8,128)} %get-tuple-element.9.dv, f32[8,128]{1,0:T(8,128)} %get-tuple-element.10.factor), custom_call_target="tpu_custom_call" | custom-call | tf_op jit(solution)/shard_map/scale/pallas_call | solution.py:422
